TPU v7x, 256 devices: a whole 4x4x8 slice. The times are simulated.
256 devices in a mesh: leaf: 4 (over y), row: 16 (over z, x_lo), col: 4 (over x_hi, core).
Axes of the slice: x: 4 (x_hi: 2, x_lo: 2; x = x_hi * 2 + x_lo), y: 4, z: 8, core: 2. Of those that a mesh axis runs over, the one named last changes fastest.
Arguments:
- rhs_top: float32 [8192, 64], P(('leaf', 'row')), may hold values from -6 to 6
- rhs_mid: float32 [8192, 64], P(('leaf', 'row')), may hold values from -6 to 6
- rhs_low: float32 [8192, 64], P(('leaf', 'row')), may hold values from -6 to 6
- inverse_top: float32 [8192, 8192], P(('leaf', 'row'), 'col'), as said below
- inverse_mid: float32 [8192, 4096], P(('leaf', 'row'), 'col'), as said below
- inverse_low: float32 [8192, 2048], P(('leaf', 'row'), 'col'), as said below
- tiles_mid: float32 [4, 16, 4, 4, 128, 128], P('leaf', 'row', 'col'), may hold values from -0.25 to 0.25
- places_mid: int32 [4, 16, 4, 4], P('leaf', 'row', 'col'), may hold values from 0 to 15, as said below
- tiles_low: float32 [4, 16, 4, 2, 128, 128], P('leaf', 'row', 'col'), may hold values from -0.375 to 0.375
- places_low: int32 [4, 16, 4, 2], P('leaf', 'row', 'col'), may hold values from 0 to 7, as said below
Outputs:
- solved_top: float32 [8192, 64], P(('leaf', 'row'))
- solved_mid: float32 [8192, 64], P(('leaf', 'row'))
- solved_low: float32 [8192, 64], P(('leaf', 'row'))
Inputs may be any that keep to these rules, and one draw needn't show every extreme that they name: `places_mid`: within one device the 4 positions are distinct, a quarter of the device's (16) x (1) tile slots. `places_low`: within one device the 2 positions are distinct, a quarter of the device's (8) x (1) tile slots. `inverse_top`: each separator's square block is lower triangular with positive diagonal. `inverse_mid`: each separator's square block is lower triangular with positive diagonal. `inverse_low`: each separator's square block is lower triangular with positive diagonal.
All inputs are finite; a program needn't handle non-finite values.
Results may differ from a plain program's by a relative error of at most 0.00014.
Values sent between devices are 32-bit elements; how exact they have to be, the bound alone decides.
A program may use at most 64 MiB of HBM per device.

v0:
```python
import jax
import jax.numpy as jnp
from jax import lax
from jax.sharding import PartitionSpec as P

highest = lax.Precision.HIGHEST


def partner(block, axis, apart):
    count = lax.axis_size(axis)
    route = []
    for low in range(count):
        high = low | 1 << apart
        if high != low and high < count:
            route += [(low, high), (high, low)]
    return lax.ppermute(block, axis, route)


def group_total(part, leaf_bits_used):
    col_size, vec_width = part.shape
    folded = part.reshape(col_size // 2, 2 * vec_width)
    share_part = lax.psum_scatter(folded, "row", scatter_dimension=0, tiled=True)
    for bit_index in range(leaf_bits_used):
        share_part = share_part + partner(share_part, "leaf", bit_index)
    summed = lax.all_gather(share_part, "row", axis=0, tiled=True)
    return summed.reshape(col_size, vec_width)


def col_total(part):
    return lax.psum(part, "col")


def col_pair(first_part, second_part):
    return lax.psum((first_part, second_part), "col")


def into_columns(own_vec, shift, col_size):
    own_count, vec_width = own_vec.shape
    padded = jnp.zeros((col_size + 2 * own_count, vec_width), jnp.float32)
    begin_at = jnp.clip(shift + own_count, 0, col_size + own_count)
    placed = lax.dynamic_update_slice_in_dim(padded, own_vec, begin_at, 0)
    return placed[own_count : own_count + col_size]


def from_columns(columns, shift, own_count):
    col_size = columns.shape[0]
    padded = jnp.pad(columns, ((own_count, own_count), (0, 0)))
    begin_at = jnp.clip(shift + own_count, 0, col_size + own_count)
    return lax.dynamic_slice_in_dim(padded, begin_at, own_count, 0)


def forward(inverse, columns):
    return jnp.dot(inverse, columns, precision=highest, preferred_element_type=jnp.float32)


def backward(inverse, own_vec):
    return lax.dot_general(
        inverse,
        own_vec,
        (((0,), (0,)), ((), ())),
        precision=highest,
        preferred_element_type=jnp.float32,
    )


def lift_tiles(tile_set, places, child_vec, col_size):
    tile_count = places.shape[-1]
    tile_size = tile_set.shape[-1]
    per_row = child_vec.shape[0] // tile_size
    squares = tile_set.reshape(tile_count, tile_size, tile_size)
    positions = places.reshape(tile_count)
    tile_row = positions // per_row
    tile_col = positions % per_row
    pieces = child_vec.reshape(per_row, tile_size, -1)[tile_col]
    product = jnp.einsum("nab,nbw->naw", squares, pieces, precision=highest)
    chooser = (
        jnp.arange(col_size // tile_size, dtype=jnp.int32)[:, None] == tile_row[None, :]
    ).astype(jnp.float32)
    return jnp.einsum("kn,naw->kaw", chooser, product, precision=highest).reshape(col_size, -1)


def lower_tiles(tile_set, places, parent_cols, own_count):
    tile_count = places.shape[-1]
    tile_size = tile_set.shape[-1]
    per_row = own_count // tile_size
    squares = tile_set.reshape(tile_count, tile_size, tile_size)
    positions = places.reshape(tile_count)
    tile_row = positions // per_row
    tile_col = positions % per_row
    pieces = parent_cols.reshape(parent_cols.shape[0] // tile_size, tile_size, -1)[tile_row]
    product = jnp.einsum("nba,nbw->naw", squares, pieces, precision=highest)
    chooser = (jnp.arange(per_row, dtype=jnp.int32)[:, None] == tile_col[None, :]).astype(
        jnp.float32
    )
    return jnp.einsum("kn,naw->kaw", chooser, product, precision=highest).reshape(own_count, -1)


def body(
    rhs_top,
    rhs_mid,
    rhs_low,
    inverse_top,
    inverse_mid,
    inverse_low,
    tiles_mid,
    places_mid,
    tiles_low,
    places_low,
):
    own_count = rhs_top.shape[0]
    leaf_count = lax.axis_size("leaf")
    leaf_bits = leaf_count.bit_length() - 1
    row_count = lax.axis_size("row")
    leaf_index = lax.axis_index("leaf")
    row_index = lax.axis_index("row")
    col_index = lax.axis_index("col")

    def placing(depth_level, col_size):
        leaf_span = leaf_count >> depth_level
        v_offset = (leaf_index % leaf_span * row_count + row_index) * own_count
        return v_offset - col_index * col_size

    size_top = inverse_top.shape[1]
    size_mid = inverse_mid.shape[1]
    size_low = inverse_low.shape[1]
    shift_top = placing(0, size_top)
    shift_mid = placing(1, size_mid)
    shift_low = placing(2, size_low)
    bits_mid = leaf_bits - 1
    bits_low = leaf_bits - 2
    base_low = group_total(into_columns(rhs_low, shift_low, size_low), bits_low)
    base_mid = group_total(into_columns(rhs_mid, shift_mid, size_mid), bits_mid)
    base_top = group_total(into_columns(rhs_top, shift_top, size_top), leaf_bits)
    low_y = col_total(forward(inverse_low, base_low))
    mid_cols = base_mid - group_total(lift_tiles(tiles_low, places_low, low_y, size_mid), bits_mid)
    mid_y = col_total(forward(inverse_mid, mid_cols))
    top_cols = base_top - group_total(lift_tiles(tiles_mid, places_mid, mid_y, size_top), leaf_bits)
    top_y = col_total(forward(inverse_top, top_cols))
    back_top = group_total(backward(inverse_top, top_y), leaf_bits)
    solved_top, down_mid = col_pair(
        from_columns(back_top, shift_top, own_count),
        lower_tiles(tiles_mid, places_mid, back_top, own_count),
    )
    back_mid = group_total(backward(inverse_mid, mid_y - down_mid), bits_mid)
    solved_mid, down_low = col_pair(
        from_columns(back_mid, shift_mid, own_count),
        lower_tiles(tiles_low, places_low, back_mid, own_count),
    )
    back_low = group_total(backward(inverse_low, low_y - down_low), bits_low)
    solved_low = col_total(from_columns(back_low, shift_low, own_count))
    return (solved_top, solved_mid, solved_low)


def solution(mesh):
    return jax.shard_map(
        body,
        mesh=mesh,
        in_specs=(
            P(("leaf", "row"), None),
            P(("leaf", "row"), None),
            P(("leaf", "row"), None),
            P(("leaf", "row"), "col"),
            P(("leaf", "row"), "col"),
            P(("leaf", "row"), "col"),
            P("leaf", "row", "col", None, None, None),
            P("leaf", "row", "col", None),
            P("leaf", "row", "col", None, None, None),
            P("leaf", "row", "col", None),
        ),
        out_specs=(P(("leaf", "row"), None), P(("leaf", "row"), None), P(("leaf", "row"), None)),
        check_vma=False,
    )
```

profile of v0, /device:TPU:1, one launch (start us, length us, event | category | flops | bytes accessed | tf_op | source)
XLA Modules:
  0.0 885.7 jit_solution(1058798755863715967)
XLA Ops:
  11.3 60.5 %reduce-scatter.13.cloned.1.call-done = f32[16,128]{1,0:T(8,128)} async-done(((f32[256,128]{1,0:T(8,128)}), f32[16,128]{1,0:T(8,128)}) %reduce-scatter.13.cloned.1.call-update) | async-done | bytes 8208 | tf_op jit(solution)/shard_map/reduce_scatter | solution.py:22
  71.8 24.7 %all_gather.26 = f32[256,128]{1,0:T(8,128)S(1)} all-gather(f32[16,128]{1,0:T(8,128)} %reduce-scatter.13.cloned.1.call-done), channel_id=1, replica_groups=mesh['leaf'=4,'row'=16,'col'=4] {'row'}, dimensions={0}, use_global_device_ids=true | all-gather | bytes 139264 | tf_op jit(solution)/shard_map/all_gather | solution.py:25
  97.2 32.0 %psum.56 = f32[128,64]{0,1:T(8,128)S(1)} all-reduce(f32[128,64]{0,1:T(8,128)S(1)} %convolution_bitcast_fusion.7), channel_id=1, replica_groups=mesh['leaf'=4,'row'=16,'col'=4] {'col'}, use_global_device_ids=true, to_apply=%region_3.4 | all-reduce | flops 8192 | bytes 65536 | tf_op jit(solution)/shard_map/psum | solution.py:30
  133.3 10.0 %reduce-scatter.11.cloned.1.call-done = f32[32,128]{1,0:T(8,128)} async-done(((f32[512,128]{1,0:T(8,128)}), f32[32,128]{1,0:T(8,128)}) %reduce-scatter.11.cloned.1.call-update) | async-done | bytes 16400 | tf_op jit(solution)/shard_map/reduce_scatter | solution.py:22
  147.2 66.3 %reduce-scatter.15.cloned.1.call-done = f32[32,128]{1,0:T(8,128)} async-done(((f32[512,128]{1,0:T(8,128)}), f32[32,128]{1,0:T(8,128)}) %reduce-scatter.15.cloned.1.call-update) | async-done | bytes 16400 | tf_op jit(solution)/shard_map/reduce_scatter | solution.py:22
  214.5 25.0 %all_gather.25 = f32[512,128]{1,0:T(8,128)S(1)} all-gather(f32[32,128]{1,0:T(8,128)S(1)} %add.158), channel_id=1, replica_groups=mesh['leaf'=4,'row'=16,'col'=4] {'row'}, dimensions={0}, use_global_device_ids=true | all-gather | bytes 278528 | tf_op jit(solution)/shard_map/all_gather | solution.py:25
  240.2 26.5 %all_gather.27 = f32[512,128]{1,0:T(8,128)S(1)} all-gather(f32[32,128]{1,0:T(8,128)S(1)} %add.160), channel_id=1, replica_groups=mesh['leaf'=4,'row'=16,'col'=4] {'row'}, dimensions={0}, use_global_device_ids=true | all-gather | bytes 278528 | tf_op jit(solution)/shard_map/all_gather | solution.py:25
  268.0 37.9 %psum.57 = f32[128,64]{0,1:T(8,128)S(1)} all-reduce(f32[128,64]{0,1:T(8,128)S(1)} %convolution_bitcast_fusion.6), channel_id=1, replica_groups=mesh['leaf'=4,'row'=16,'col'=4] {'col'}, use_global_device_ids=true, to_apply=%region_5.6 | all-reduce | flops 8192 | bytes 65536 | tf_op jit(solution)/shard_map/psum | solution.py:30
  312.4 2.8 collective-permute-start.1
  315.3 52.2 %reduce-scatter.17.cloned.1.call-done = f32[64,128]{1,0:T(8,128)} async-done(((f32[1024,128]{1,0:T(8,128)}), f32[64,128]{1,0:T(8,128)}) %reduce-scatter.17.cloned.1.call-update) | async-done | bytes 32784 | tf_op jit(solution)/shard_map/reduce_scatter | solution.py:22
  371.6 2.7 collective-permute-start.5
  374.3 26.6 %all_gather.24 = f32[1024,128]{1,0:T(8,128)S(1)} all-gather(f32[64,128]{1,0:T(8,128)S(1)} %add.154), channel_id=1, replica_groups=mesh['leaf'=4,'row'=16,'col'=4] {'row'}, dimensions={0}, use_global_device_ids=true | all-gather | bytes 557056 | tf_op jit(solution)/shard_map/all_gather | solution.py:25
  400.9 27.0 %all_gather.28 = f32[1024,128]{1,0:T(8,128)S(1)} all-gather(f32[64,128]{1,0:T(8,128)S(1)} %add.162), channel_id=1, replica_groups=mesh['leaf'=4,'row'=16,'col'=4] {'row'}, dimensions={0}, use_global_device_ids=true | all-gather | bytes 557056 | tf_op jit(solution)/shard_map/all_gather | solution.py:25
  430.0 40.2 %psum.58 = f32[128,64]{0,1:T(8,128)S(1)} all-reduce(f32[128,64]{0,1:T(8,128)S(1)} %convolution_bitcast_fusion.5), channel_id=1, replica_groups=mesh['leaf'=4,'row'=16,'col'=4] {'col'}, use_global_device_ids=true, to_apply=%region_7.8 | all-reduce | flops 8192 | bytes 65536 | tf_op jit(solution)/shard_map/psum | solution.py:30
  472.3 56.4 %reduce-scatter.19.cloned.1.call-done = f32[64,128]{1,0:T(8,128)} async-done(((f32[1024,128]{1,0:T(8,128)}), f32[64,128]{1,0:T(8,128)}) %reduce-scatter.19.cloned.1.call-update) | async-done | bytes 32784 | tf_op jit(solution)/shard_map/reduce_scatter | solution.py:22
  532.8 2.7 collective-permute-start.7
  537.1 26.5 %all_gather.29 = f32[1024,128]{1,0:T(8,128)S(1)} all-gather(f32[64,128]{1,0:T(8,128)S(1)} %add.164), channel_id=1, replica_groups=mesh['leaf'=4,'row'=16,'col'=4] {'row'}, dimensions={0}, use_global_device_ids=true | all-gather | bytes 557056 | tf_op jit(solution)/shard_map/all_gather | solution.py:25
  567.0 33.4 %psum.60 = f32[128,64]{0,1:T(8,128)S(1)} all-reduce(f32[128,64]{0,1:T(8,128)S(1)} %bitcast.66), channel_id=1, replica_groups=mesh['leaf'=4,'row'=16,'col'=4] {'col'}, use_global_device_ids=true, to_apply=%region_10.11 | all-reduce | flops 8192 | bytes 65536 | tf_op jit(solution)/shard_map/psum | solution.py:34
  602.7 58.2 %reduce-scatter.21.cloned.1.call-done = f32[32,128]{1,0:T(8,128)} async-done(((f32[512,128]{1,0:T(8,128)}), f32[32,128]{1,0:T(8,128)}) %reduce-scatter.21.cloned.1.call-update) | async-done | bytes 16400 | tf_op jit(solution)/shard_map/reduce_scatter | solution.py:22
  664.9 25.6 %all_gather.30 = f32[512,128]{1,0:T(8,128)S(1)} all-gather(f32[32,128]{1,0:T(8,128)S(1)} %add.166), channel_id=1, replica_groups=mesh['leaf'=4,'row'=16,'col'=4] {'row'}, dimensions={0}, use_global_device_ids=true | all-gather | bytes 278528 | tf_op jit(solution)/shard_map/all_gather | solution.py:25
  691.8 32.3 %psum.62 = f32[128,64]{0,1:T(8,128)S(1)} all-reduce(f32[128,64]{0,1:T(8,128)S(1)} %bitcast.67), channel_id=1, replica_groups=mesh['leaf'=4,'row'=16,'col'=4] {'col'}, use_global_device_ids=true, to_apply=%region_13.14 | all-reduce | flops 8192 | bytes 65536 | tf_op jit(solution)/shard_map/psum | solution.py:34
  727.0 56.7 %reduce-scatter.23.cloned.1.call-done = f32[16,128]{1,0:T(8,128)} async-done(((f32[256,128]{1,0:T(8,128)}), f32[16,128]{1,0:T(8,128)}) %reduce-scatter.23.cloned.1.call-update) | async-done | bytes 8208 | tf_op jit(solution)/shard_map/reduce_scatter | solution.py:22
  783.7 24.6 %all_gather.31 = f32[256,128]{1,0:T(8,128)S(1)} all-gather(f32[16,128]{1,0:T(8,128)} %reduce-scatter.23.cloned.1.call-done), channel_id=1, replica_groups=mesh['leaf'=4,'row'=16,'col'=4] {'row'}, dimensions={0}, use_global_device_ids=true | all-gather | bytes 139264 | tf_op jit(solution)/shard_map/all_gather | solution.py:25
  809.0 65.5 %all-reduce.6.cloned.1.call-done = (f32[128,64]{1,0:T(8,128)}, f32[128,64]{1,0:T(8,128)}, f32[128,64]{1,0:T(8,128)}) async-done(((f32[128,64]{1,0:T(8,128)}, f32[128,64]{1,0:T(8,128)}, f32[128,64]{1,0:T(8,128)}), (f32[128,64]{1,0:T(8,128)}, f32[128,64]{1,0:T(8,128)}, f32[128,64]{1,0:T(8,128)})) %all-reduce.6.cloned.1.call-update) | async-done | bytes 98320 | tf_op jit(solution)/shard_map/psum | solution.py:34
  (132 shorter events, 55.1 us)
Async XLA Ops:
  7.2 421.0 %copy-start = (f32[128,2048]{1,0:T(8,128)S(1)}, f32[128,2048]{1,0:T(8,128)}, u32[]{:S(2)}) copy-start(f32[128,2048]{1,0:T(8,128)} %param.13) | copy-start | bytes 3145732
  7.2 64.7 %reduce-scatter.13.cloned.1.call-start = ((), (), s32[]{:S(2)}) async-start(), calls=%async_computation.10 | async-start | bytes 139264 | tf_op jit(solution)/shard_map/reduce_scatter | solution.py:22
  9.5 133.7 %reduce-scatter.11.cloned.1.call-start = ((), (), s32[]{:S(2)}) async-start(), calls=%async_computation.9 | async-start | bytes 278528 | tf_op jit(solution)/shard_map/reduce_scatter | solution.py:22
  10.4 118.9 %copy-start.5 = (f32[1,1,1,2,128,128]{5,4,3,2,1,0:T(8,128)S(1)}, f32[1,1,1,2,128,128]{5,4,3,2,1,0:T(8,128)}, u32[]{:S(2)}) copy-start(f32[1,1,1,2,128,128]{5,4,3,2,1,0:T(8,128)} %param.18) | copy-start | bytes 393220
  10.4 119.4 %copy-start.11 = (s32[1,1,1,2]{3,2,1,0:T(1,128)S(1)}, s32[1,1,1,2]{3,2,1,0:T(1,128)}, u32[]{:S(2)}) copy-start(s32[1,1,1,2]{3,2,1,0:T(1,128)} %param.19) | copy-start | bytes 28
  11.3 202.2 %reduce-scatter.15.cloned.1.call-start = ((), (), s32[]{:S(2)}) async-start(), calls=%async_computation.11 | async-start | bytes 278528 | tf_op jit(solution)/shard_map/reduce_scatter | solution.py:22
  131.3 177.3 %reduce-scatter.9.cloned.1.call-start = ((), (), s32[]{:S(2)}) async-start(), calls=%async_computation.8 | async-start | bytes 557056 | tf_op jit(solution)/shard_map/reduce_scatter | solution.py:22
  133.2 133.7 %copy-start.1 = (f32[128,1024]{1,0:T(8,128)S(1)}, f32[128,1024]{1,0:T(8,128)}, u32[]{:S(2)}) copy-start(f32[128,1024]{1,0:T(8,128)} %param.14) | copy-start | bytes 1572868
  133.2 234.2 %reduce-scatter.17.cloned.1.call-start = ((), (), s32[]{:S(2)}) async-start(), calls=%async_computation.12 | async-start | bytes 557056 | tf_op jit(solution)/shard_map/reduce_scatter | solution.py:22
  143.2 3.2 collective-permute-start.2
  213.5 26.0 %collective-permute-start.3 = (f32[32,128]{1,0:T(8,128)}, f32[32,128]{1,0:T(8,128)S(1)}, u32[]{:S(2)}, u32[]{:S(2)}) collective-permute-start(f32[32,128]{1,0:T(8,128)} %reduce-scatter.15.cloned.1.call-done), channel_id=1, source_target_pairs={{0,64},{64,0},{128,192},{192,128},{1,65},{65,1},{129,193},{193,129... | collective-permute-start | bytes 49160 | tf_op jit(solution)/shard_map/ppermute | solution.py:16
  308.5 220.1 %reduce-scatter.19.cloned.1.call-start = ((), (), s32[]{:S(2)}) async-start(), calls=%async_computation.13 | async-start | bytes 557056 | tf_op jit(solution)/shard_map/reduce_scatter | solution.py:22
  308.6 3.1 collective-permute-start
  312.4 56.2 %collective-permute-start.1 = (f32[64,128]{1,0:T(8,128)S(1)}, f32[64,128]{1,0:T(8,128)S(1)}, u32[]{:S(2)}, u32[]{:S(2)}) collective-permute-start(f32[64,128]{1,0:T(8,128)S(1)} %add.153), channel_id=1, source_target_pairs={{0,128},{128,0},{64,192},{192,64},{1,129},{129,1},{65,193},{193,65... | collective-permute-start | bytes 98312 | tf_op jit(solution)/shard_map/ppermute | solution.py:16
  367.4 3.4 collective-permute-start.4
  371.6 29.3 %collective-permute-start.5 = (f32[64,128]{1,0:T(8,128)S(1)}, f32[64,128]{1,0:T(8,128)S(1)}, u32[]{:S(2)}, u32[]{:S(2)}) collective-permute-start(f32[64,128]{1,0:T(8,128)S(1)} %add.161), channel_id=1, source_target_pairs={{0,128},{128,0},{64,192},{192,64},{1,129},{129,1},{65,193},{193,65... | collective-permute-start | bytes 98312 | tf_op jit(solution)/shard_map/ppermute | solution.py:16
  472.2 188.7 %reduce-scatter.21.cloned.1.call-start = ((), (), s32[]{:S(2)}) async-start(), calls=%async_computation.14 | async-start | bytes 278528 | tf_op jit(solution)/shard_map/reduce_scatter | solution.py:22
  528.7 3.4 collective-permute-start.6
  532.8 4.3 collective-permute-start.7
  602.6 121.5 %copy-start.4 = (f32[128,512]{1,0:T(8,128)S(1)}, f32[128,512]{1,0:T(8,128)}, u32[]{:S(2)}) copy-start(f32[128,512]{1,0:T(8,128)} %param.15) | copy-start | bytes 786436
  602.6 121.5 %copy-start.7 = (f32[128,64]{0,1:T(8,128)S(1)}, f32[128,64]{0,1:T(8,128)}, u32[]{:S(2)}) copy-start(f32[128,64]{0,1:T(8,128)} %copy-done.6) | copy-start | bytes 98308
  602.6 181.1 %reduce-scatter.23.cloned.1.call-start = ((), (), s32[]{:S(2)}) async-start(), calls=%async_computation.15 | async-start | bytes 139264 | tf_op jit(solution)/shard_map/reduce_scatter | solution.py:22
  660.9 3.2 collective-permute-start.8
  725.2 149.3 %all-reduce.6.cloned.1.call-start = ((), (), s32[]{:S(2)}) async-start(), calls=%async_computation.16 | async-start | bytes 393216 | tf_op jit(solution)/shard_map/psum | solution.py:34
  (7 other events, 171.2 us)
Sparse Core Ops, SparseCore 0:
  10.5 61.2 reduce-scatter.12
  74.5 68.7 reduce-scatter.10
  145.7 67.6 reduce-scatter.14
  216.0 69.3 reduce-scatter.8
  308.7 58.7 reduce-scatter.16
  472.3 56.3 reduce-scatter.18
  602.8 58.1 reduce-scatter.20
  725.4 58.2 reduce-scatter.22
  809.2 65.3 all-reduce.5
where the time goes:
time: 887 us; the launch traced here: 886 us
  waiting for transfers between devices  438 us (49%)
  blocking collectives  382 us (43%)
  local copies, waits for them, and re-layouts  21.3 us (2%)
  starting transfers between devices  15.7 us (2%)
  between operations  14.4 us (2%)
  matrix products  9.91 us (1%)
    reduce_scatter x8, waiting for transfers between devices, group_total(): lax.psum_scatter(folded, 'row', scatter_dimension=0, tiled=True)  360 us
    all_gather x8, blocking collectives, group_total(): summed = lax.all_gather(share_part, 'row', axis=0, tiled=True)  206 us
    psum x3, blocking collectives, col_total(): return lax.psum(part, 'col')  110 us
    psum x2, blocking collectives, col_pair(): return lax.psum((first_part, second_part), 'col')  65.7 us
    psum x1, waiting for transfers between devices, col_pair(): return lax.psum((first_part, second_part), 'col')  65.5 us
  transfers between devices with their start and end apart: 18, of which 14 were waited for; matrix products, arithmetic and copies ran while one was open for 2% of the time, Pallas kernels for 0%

commit v1 on v0

v1 whole, which is shorter than its diff:
```python
import functools

import jax
import jax.numpy as jnp
from jax import lax
from jax.experimental import pallas as pl
from jax.experimental.pallas import tpu as pltpu
from jax.sharding import PartitionSpec as P

MESH = pl.DeviceIdType.MESH
TILE = 128
BATCHES = 2
N_LEAF, N_Z, N_X, N_COL = 4, 8, 2, 4
N_ROW = N_Z * N_X
BLOCK = 8
bf16 = jnp.bfloat16
f32 = jnp.float32


def outward(count):
    middle = count // 2
    return [(middle + (-1 if j % 2 else 1) * ((j + 1) // 2)) % count for j in range(count)]


def split(a):
    high = a.astype(bf16)
    return high, (a - high.astype(f32)).astype(bf16)


def product(a, high, low):
    width = a.shape[0]
    a_high, a_low = split(a)
    both = jnp.dot(jnp.concatenate([a_high, a_low], axis=0), high, preferred_element_type=f32)
    return both[:width] + both[width:] + jnp.dot(a_high, low, preferred_element_type=f32)


def kernel(
    rhs_top, rhs_mid, rhs_low, inv_top, inv_mid, inv_low, tiles_mid, places_mid, tiles_low, places_low,
    out_top, out_mid, out_low,
    rt, rm, rl, it, im, il, tm, tl,
    rtt, rmt, rlt,
    top_h, top_l, topt_h, topt_l, mid_h, mid_l, midt_h, midt_l, low_h, low_l, lowt_h, lowt_l,
    tm_h, tm_l, tmt_h, tmt_l, tl_h, tl_l, tlt_h, tlt_l,
    x_low,
    send1, got1, x_mid, send2, got2, x_top, send3, got3, s_top_0, s_top_1, send4, got4, s_mid_0, s_mid_1, send5, got5, tail5,
    col_got, low_y, mid_y,
    o_top, o_mid, o_low,
    load_sem, start_sem, start_out, rs_sem, rs_out, ag_sem, ag_out, col_sem, col_out, res_sem, res_out, end_sem, end_out,
):
    width = 64 // BATCHES
    per_tile = width // BLOCK
    leaf = lax.axis_index("leaf")
    row = lax.axis_index("row")
    col = lax.axis_index("col")
    z = row // N_X
    x = lax.rem(row, N_X)

    rows_at = {}
    for dz in range(N_Z):
        for dx in range(N_X):
            rows_at[dz, dx] = lax.rem(z + dz, N_Z) * N_X + lax.rem(x + dx, N_X)
    pair = leaf // 2 * 2

    def peers(kind):
        if kind == "top":
            leaves = [(lax.rem(leaf + dy, N_LEAF), dy) for dy in outward(N_LEAF)]
        elif kind == "mid":
            leaves = [(pair + lax.rem(leaf - pair + dy, 2), dy) for dy in (1, 0)]
        else:
            leaves = [(leaf, 0)]
        found = []
        for other, dy in leaves:
            for dz in outward(N_Z):
                for dx in (1, 0):
                    if (dy, dz, dx) != (0, 0, 0):
                        r = rows_at[dz, dx]
                        base = {"top": other, "mid": other - pair, "low": 0}[kind]
                        found.append((base * N_ROW + r, (other, r, col)))
        return found

    group = {k: peers(k) for k in ("top", "mid", "low")}
    own = {"top": leaf * N_ROW + row, "mid": (leaf - pair) * N_ROW + row, "low": row}
    others = [(leaf, row, lax.rem(col + d, N_COL)) for d in (2, 3, 1)]

    target_row = col * 4 + row // 4
    source_col = row // 4
    source_row = lax.rem(row, 4) * 4

    def remote(src, dst, send, recv, device):
        return pltpu.make_async_remote_copy(
            src_ref=src, dst_ref=dst, send_sem=send, recv_sem=recv, device_id=device, device_id_type=MESH
        )

    loads = [
        pltpu.make_async_copy(src, dst, load_sem.at[i])
        for i, (src, dst) in enumerate(
            [
                (rhs_low, rl),
                (inv_low, il),
                (tiles_low.at[0, 0, 0], tl),
                (rhs_mid, rm),
                (inv_mid, im),
                (tiles_mid.at[0, 0, 0], tm),
                (rhs_top, rt),
                (inv_top, it),
            ]
        )
    ]
    for load in loads:
        load.start()

    barrier = pltpu.get_barrier_semaphore()
    for _, device in group["top"]:
        pl.semaphore_signal(barrier, inc=1, device_id=device, device_id_type=MESH)
    for device in others:
        pl.semaphore_signal(barrier, inc=1, device_id=device, device_id_type=MESH)
    for i in range(4):
        source = (leaf, source_row + i, source_col)

        @pl.when(jnp.logical_or(source_row + i != row, source_col != col))
        def _():
            pl.semaphore_signal(barrier, inc=1, device_id=source, device_id_type=MESH)

    self_target = (target_row == row).astype(jnp.int32)

    def keep(ref, value):
        for b in range(BATCHES):
            ref[b] = value[b * width : (b + 1) * width].reshape(per_tile, BLOCK, TILE)

    def prepare(raw, high, low, high_t, low_t):
        for p in range(raw.shape[1] // TILE):
            cut = slice(p * TILE, (p + 1) * TILE)
            block = raw[:, cut]
            high[:, cut], low[:, cut] = split(block)
            high_t[cut, :], low_t[cut, :] = split(block.T)

    def prepare_tiles(raw, high, low, high_t, low_t):
        for n in range(raw.shape[0]):
            block = raw[n]
            high[n], low[n] = split(block)
            high_t[n], low_t[n] = split(block.T)

    loads[0].wait()
    keep(rlt, rl[...])
    pl.semaphore_wait(barrier, len(group["top"]) + len(others) + 4 - self_target)

    is_source = col == row // 4
    place_low = lax.rem(row, 4) * per_tile

    @pl.when(is_source)
    def _():
        for b in range(BATCHES):
            here = x_low.at[b, pl.ds(place_low, per_tile)]
            for _, device in group["low"]:
                remote(rlt.at[b], here, start_out.at[b], start_sem.at[b], device).start()
            pltpu.make_async_copy(rlt.at[b], here, start_sem.at[b]).start()

    loads[1].wait()
    prepare(il, low_h, low_l, lowt_h, lowt_l)

    def batch(ref, b):
        return ref[b] if isinstance(ref, tuple) else ref.at[b]

    def whole(ref, sem):
        return pltpu.make_async_copy(ref, ref, sem)

    def columns(ref, b, positions):
        return jnp.concatenate(
            [batch(ref, b)[p * per_tile : (p + 1) * per_tile].reshape(width, TILE) for p in range(positions)],
            axis=1,
        )

    def forward(ref, b, positions, high_t, low_t):
        return product(columns(ref, b, positions), high_t[...], low_t[...])

    def send_col(stage, b, value):
        col_got[stage, b, col] = value
        for device in others:
            mine = col_got.at[stage, b, col]
            remote(mine, mine, col_out.at[stage, b], col_sem.at[stage, b], device).start()

    def get_col(stage, b):
        whole(col_got.at[stage, b, pl.ds(0, N_COL - 1)], col_sem.at[stage, b]).wait()
        got = [col_got[stage, b, c] for c in range(N_COL)]
        return (got[0] + got[1]) + (got[2] + got[3])

    def send_shares(stage, b, kind, send, got):
        me = own[kind]
        for k, device in group[kind]:
            remote(send.at[b, k], got.at[b, me], rs_out.at[stage, b], rs_sem.at[stage, b], device).start()
        got[b, me] = send[b, me]

    def sum_shares(stage, b, kind, got):
        whole(got.at[b, pl.ds(0, len(group[kind]))], rs_sem.at[stage, b]).wait()
        return jnp.sum(got[b], axis=0)

    def spread(stage, b, kind, total, ref):
        mine = batch(ref, b).at[own[kind]]
        mine[...] = total
        for _, device in group[kind]:
            remote(mine, mine, ag_out.at[stage, b], ag_sem.at[stage, b], device).start()

    def get_columns(stage, b, kind, ref):
        whole(batch(ref, b).at[pl.ds(0, len(group[kind]))], ag_sem.at[stage, b]).wait()

    def lift(vector, b, places, high_t, low_t, rhs_t, is_mine, my_place, send, positions):
        rhs = jnp.where(is_mine, rhs_t[b].reshape(width, TILE), 0.0)
        parts = [product(vector, high_t[n], low_t[n]) for n in range(high_t.shape[0])]
        for p in range(positions):
            value = jnp.where(my_place == p, rhs, 0.0)
            for n, part in enumerate(parts):
                value = value - jnp.where(places[0, 0, 0, n] == p, part, 0.0)
            send[b, p * per_tile : (p + 1) * per_tile] = value.reshape(per_tile, BLOCK, TILE)

    def lower(ref, b, places, high, low):
        total = None
        for n in range(high.shape[0]):
            place = places[0, 0, 0, n] * per_tile
            picked = jnp.concatenate([batch(ref, b)[place + q] for q in range(per_tile)], axis=0)
            part = product(picked, high[n], low[n])
            total = part if total is None else total + part
        return total

    def backward(value, b, high, low, send):
        for p in range(high.shape[1] // TILE):
            cut = slice(p * TILE, (p + 1) * TILE)
            part = product(value, high[:, cut], low[:, cut])
            send[b, p * per_tile : (p + 1) * per_tile] = part.reshape(per_tile, BLOCK, TILE)

    mid_index = (leaf - pair) * N_ROW + row
    mine_mid, place_mid = col == mid_index // 8, lax.rem(mid_index, 8)
    mine_top, place_top = col == leaf, row

    def send_result(level, b, ref, mine, place, out):
        @pl.when(mine)
        def _():
            src = batch(ref, b).at[pl.ds(place * per_tile, per_tile)]
            for device in others:
                remote(src, out.at[b], res_out.at[level, b], res_sem.at[level, b], device).start()
            pltpu.make_async_copy(src, out.at[b], res_sem.at[level, b]).start()

    def finish(ref, out):
        out[...] = ref[...].reshape(64, TILE)

    every = range(BATCHES)
    s_top, s_mid = (s_top_0, s_top_1), (s_mid_0, s_mid_1)
    for b in every:
        whole(x_low.at[b], start_sem.at[b]).wait()
        send_col(0, b, forward(x_low, b, 4, lowt_h, lowt_l))
    loads[2].wait()
    prepare_tiles(tl, tl_h, tl_l, tlt_h, tlt_l)
    loads[3].wait()
    keep(rmt, rm[...])
    for b in every:
        low_y[b] = get_col(0, b)
        lift(low_y[b], b, places_low, tlt_h, tlt_l, rmt, mine_mid, place_mid, send1, 8)
        send_shares(0, b, "mid", send1, got1)
    loads[4].wait()
    prepare(im, mid_h, mid_l, midt_h, midt_l)
    for b in every:
        spread(0, b, "mid", sum_shares(0, b, "mid", got1), x_mid)
    loads[5].wait()
    prepare_tiles(tm, tm_h, tm_l, tmt_h, tmt_l)
    loads[6].wait()
    keep(rtt, rt[...])
    for b in every:
        get_columns(0, b, "mid", x_mid)
        send_col(1, b, forward(x_mid, b, 8, midt_h, midt_l))
    for b in every:
        mid_y[b] = get_col(1, b)
        lift(mid_y[b], b, places_mid, tmt_h, tmt_l, rtt, mine_top, place_top, send2, 16)
        send_shares(1, b, "top", send2, got2)
    loads[7].wait()
    prepare(it, top_h, top_l, topt_h, topt_l)
    for b in every:
        spread(1, b, "top", sum_shares(1, b, "top", got2), x_top)
    for b in every:
        get_columns(1, b, "top", x_top)
        send_col(2, b, forward(x_top, b, 16, topt_h, topt_l))
    for b in every:
        backward(get_col(2, b), b, top_h, top_l, send3)
        send_shares(2, b, "top", send3, got3)
    for b in every:
        spread(2, b, "top", sum_shares(2, b, "top", got3), s_top)
    for b in every:
        get_columns(2, b, "top", s_top)
        send_col(3, b, lower(s_top, b, places_mid, tm_h, tm_l))
        send_result(0, b, s_top, mine_top, place_top, o_top)
    for b in every:
        backward(mid_y[b] - get_col(3, b), b, mid_h, mid_l, send4)
        send_shares(3, b, "mid", send4, got4)
    for b in every:
        spread(3, b, "mid", sum_shares(3, b, "mid", got4), s_mid)
    for b in every:
        get_columns(3, b, "mid", s_mid)
        send_col(4, b, lower(s_mid, b, places_low, tl_h, tl_l))
        send_result(1, b, s_mid, mine_mid, place_mid, o_mid)
    for b in every:
        backward(low_y[b] - get_col(4, b), b, low_h, low_l, send5)
        send_shares(4, b, "low", send5, got5)
    slot = lax.rem(row, 4)
    for b in every:
        tail5[b] = sum_shares(4, b, "low", got5)
        for c in range(N_COL):
            to_self = jnp.logical_and(col == c, target_row == row)

            @pl.when(to_self)
            def _():
                pltpu.make_async_copy(tail5.at[b], o_low.at[b, slot], end_sem.at[b]).start()

            @pl.when(jnp.logical_not(to_self))
            def _():
                remote(
                    tail5.at[b], o_low.at[b, slot], end_out.at[b], end_sem.at[b], (leaf, target_row, c)
                ).start()

    for level, (ref, out) in enumerate([(o_top, out_top), (o_mid, out_mid)]):
        for b in every:
            whole(ref.at[b], res_sem.at[level, b]).wait()
        finish(ref, out)
    for b in every:
        whole(o_low.at[b], end_sem.at[b]).wait()
    finish(o_low, out_low)

    for b in every:

        @pl.when(is_source)
        def _():
            for _ in group["low"]:
                whole(rlt.at[b], start_out.at[b]).wait()

        for level, mine in enumerate([mine_top, mine_mid]):

            @pl.when(mine)
            def _():
                for _ in others:
                    whole(o_top.at[b], res_out.at[level, b]).wait()

        for stage, (kind, send, ref) in enumerate(
            [
                ("mid", send1, x_mid),
                ("top", send2, x_top),
                ("top", send3, s_top),
                ("mid", send4, s_mid),
                ("low", send5, None),
            ]
        ):
            count = len(group[kind])
            whole(send.at[b, pl.ds(0, count)], rs_out.at[stage, b]).wait()
            if ref is not None:
                whole(batch(ref, b).at[pl.ds(0, count)], ag_out.at[stage, b]).wait()
            whole(col_got.at[stage, b, pl.ds(0, N_COL - 1)], col_out.at[stage, b]).wait()
        for c in range(N_COL):

            @pl.when(jnp.logical_not(jnp.logical_and(col == c, target_row == row)))
            def _():
                whole(tail5.at[b], end_out.at[b]).wait()


def body(rhs_top, rhs_mid, rhs_low, *others):
    width = 64 // BATCHES
    per_tile = width // BLOCK
    vm = pltpu.VMEM

    def blocks(count):
        return vm((BATCHES, count, BLOCK, TILE), f32)

    def alone(count):
        return vm((count, BLOCK, TILE), f32)

    def halves(*shape):
        return [vm(shape, bf16)] * 2

    rhs = [vm((64, TILE), f32)] * 3
    scratch = rhs + [
        vm((128, 2048), f32), vm((128, 1024), f32), vm((128, 512), f32), vm((4, 128, 128), f32), vm((2, 128, 128), f32),
    ]
    scratch += [blocks(per_tile)] * 3
    for size in (2048, 1024, 512):
        scratch += halves(128, size) + halves(size, 128)
    for count in (4, 2):
        scratch += halves(count, 128, 128) * 2
    scratch += [blocks(4 * per_tile)]
    scratch += [blocks(32)] * 3 + [blocks(64)] * 5 + [alone(64)] * 2 + [blocks(32)] * 2 + [alone(32)] * 2
    scratch += [blocks(16)] * 2 + [vm((BATCHES, BLOCK, TILE), f32)]
    scratch += [vm((5, BATCHES, N_COL, width, TILE), f32)] + [vm((BATCHES, width, TILE), f32)] * 2
    scratch += [blocks(per_tile)] * 3
    dma = pltpu.SemaphoreType.DMA
    scratch += [
        dma((8,)), dma((BATCHES,)), dma((BATCHES,)), dma((5, BATCHES)), dma((5, BATCHES)), dma((4, BATCHES)),
        dma((4, BATCHES)), dma((5, BATCHES)), dma((5, BATCHES)), dma((2, BATCHES)), dma((2, BATCHES)),
        dma((BATCHES,)), dma((BATCHES,)),
    ]
    anywhere = pl.BlockSpec(memory_space=pltpu.HBM)
    scalars = pl.BlockSpec(memory_space=pltpu.SMEM)
    out = pl.BlockSpec(memory_space=pltpu.VMEM)
    solved = pl.pallas_call(
        kernel,
        name="solve",
        out_shape=[jax.ShapeDtypeStruct((64, TILE), f32)] * 3,
        in_specs=[anywhere] * 7 + [scalars, anywhere, scalars],
        out_specs=[out] * 3,
        scratch_shapes=scratch,
        compiler_params=pltpu.CompilerParams(
            collective_id=0, has_side_effects=True, vmem_limit_bytes=60 * 1024 * 1024
        ),
    )(rhs_top.T, rhs_mid.T, rhs_low.T, *others)
    return tuple(part.T for part in solved)


def solution(mesh):
    vector = P(("leaf", "row"), None)
    matrix = P(("leaf", "row"), "col")
    tiles = P("leaf", "row", "col", None, None, None)
    places = P("leaf", "row", "col", None)
    return jax.shard_map(
        body,
        mesh=mesh,
        in_specs=(vector, vector, vector, matrix, matrix, matrix, tiles, places, tiles, places),
        out_specs=(vector, vector, vector),
        check_vma=False,
    )
```

time: 887 us -> 127 us (0.14)
  waiting for transfers between devices: 438 us -> 0 us
  blocking collectives: 382 us -> 0 us
  Pallas kernels: 0 us -> 123 us
  local copies, waits for them, and re-layouts: 21.3 us -> 2.77 us
  starting transfers between devices: 15.7 us -> 0 us
  between operations: 14.4 us -> 0.65 us
  matrix products: 9.91 us -> 0 us
    reduce_scatter x8 -> x0, waiting for transfers between devices: 360 us -> none  [group_total(): lax.psum_scatter(folded, 'row', scatter_dimension=0, tiled=True)]
    all_gather x8 -> x0, blocking collectives: 206 us -> none  [group_total(): summed = lax.all_gather(share_part, 'row', axis=0, tiled=True)]
    psum x5 -> x0, blocking collectives: 176 us -> none  [the longest x3 110 us: col_total(): return lax.psum(part, 'col')]
    pallas_call x0 -> x1, Pallas kernels: none -> 123 us  [body(): pl.pallas_call(kernel, name='solve', out_shape=[jax.ShapeDtypeStruct((64,...]
    psum x1 -> x0, waiting for transfers between devices: 65.5 us -> none  [col_pair(): return lax.psum((first_part, second_part), 'col')]
    ppermute x9 -> x0, starting transfers between devices: 15.4 us -> none  [partner(): return lax.ppermute(block, axis, route)]
    ppermute x9 -> x0, waiting for transfers between devices: 11.7 us -> none  [partner(): return lax.ppermute(block, axis, route)]
    dot_general x14 -> x0, matrix products: 9.91 us -> none  [the longest x3 3.41 us: forward(): jnp.dot(inverse, columns, precision=highest, preferred_element_type=jnp.f...]
  transfers between devices with their start and end apart: 18 -> 0, of which waited for: 14 -> 0; matrix products, arithmetic and copies ran while one was open for 2% -> 0% of each run, Pallas kernels for 0% -> 0%
where the time goes in v1:
time: 127 us
  Pallas kernels  123 us (97%)
  local copies, waits for them, and re-layouts  2.77 us (2%)
    pallas_call x1, Pallas kernels, body(): pl.pallas_call(kernel, name='solve', out_shape=[jax.ShapeDtypeStruct((64,...  123 us
    unnamed x7, local copies, waits for them, and re-layouts  2.77 us

profile of v1, /device:TPU:1, one launch (start us, length us, event | category | flops | bytes accessed | tf_op | source)
XLA Modules:
  0.0 126.7 jit_solution(16631343711592975684)
XLA Ops:
  0.6 123.3 %solve.1 = (f32[64,128]{1,0:T(8,128)}, f32[64,128]{1,0:T(8,128)}, f32[64,128]{1,0:T(8,128)}) custom-call(f32[64,128]{1,0:T(8,128)} %bitcast.6, f32[64,128]{1,0:T(8,128)} %bitcast.7, f32[64,128]{1,0:T(8,128)} %bitcast.8, f32[128,2048]{1,0:T(8,128)} %inv_top.1, f32[128,1024]{1,0:T(8,128)} %inv_mid.1, f32[128,512]{1,0:T(8,128)} %inv_low.1, ...), custom_call_target="tpu_custom_call" | custom-call | tf_op jit(solution)/shard_map/solve/pallas_call | solution.py:397
  123.9 0.0 copy-start.1
  123.9 1.4 %copy.16 = f32[128,64]{0,1:T(8,128)} copy(f32[128,64]{0,1:T(8,128)} %bitcast.11) | data formatting | bytes 65536
  125.3 0.0 copy-done.1
  125.3 0.0 copy-start
  125.3 0.6 copy.17
  125.9 0.2 copy-done
  126.1 0.6 copy.18
Async XLA Ops:
  123.9 1.4 %copy-start.1 = (f32[64,128]{1,0:T(8,128)S(1)}, f32[64,128]{1,0:T(8,128)}, u32[]{:S(2)}) copy-start(f32[64,128]{1,0:T(8,128)} %get-tuple-element.7) | copy-start | bytes 98308
  125.3 0.8 copy-start

commit v2 on v1

v2 whole, which is shorter than its diff:
```python
import jax
import jax.numpy as jnp
from jax import lax
from jax.experimental import pallas as pl
from jax.experimental.pallas import tpu as pltpu
from jax.sharding import PartitionSpec as P

MESH = pl.DeviceIdType.MESH
TILE = 128
BATCHES = 2
N_LEAF, N_Z, N_X, N_COL = 4, 8, 2, 4
N_ROW = N_Z * N_X
SHARE = 64 // N_COL
BLOCK = SHARE // BATCHES
bf16 = jnp.bfloat16
f32 = jnp.float32
TOP, MID, LOW = 64, 32, 16
PIECES = 2
NN = (((1,), (0,)), ((), ()))
NT = (((1,), (1,)), ((), ()))


def outward(count):
    middle = count // 2
    return [(middle + (-1 if j % 2 else 1) * ((j + 1) // 2)) % count for j in range(count)]


def split(a):
    high = a.astype(bf16)
    return high, (a - high.astype(f32)).astype(bf16)


def product(a, high, low, dims):
    width = a.shape[0]
    a_high = a.astype(bf16).astype(f32)
    both = jnp.concatenate([a_high, a - a_high], axis=0).astype(bf16)
    one = lax.dot_general(both, high, dims, preferred_element_type=f32)
    two = lax.dot_general(both, low, dims, preferred_element_type=f32)
    return (one[:width] + one[width:]) + (two[:width] + two[width:])


def kernel(
    rhs_top, rhs_mid, rhs_low, inv_top, inv_mid, inv_low, tiles_mid, places_mid, tiles_low, places_low,
    out_top, out_mid, out_low,
    rt, rm, rl, rt_cut, rm_cut, rl_cut,
    it, im, il, tm, tl, all_mid, all_low,
    top_h, top_l, mid_h, mid_l, low_h, low_l, own_mid_h, own_mid_l, own_low_h, own_low_l,
    tm_h, tm_l, tl_h, tl_l, own_tm_h, own_tm_l, own_tl_h, own_tl_l,
    x_low, send1, got1, x_mid, send2, got2, x_top, send3, got3, s_top_0, s_top_1, send4, got4, s_mid_0, s_mid_1,
    send5, got5, tail5, col_got, low_y, mid_y, o_top, o_mid, o_low,
    load_sem, place_sem, place_out, start_sem, start_out, rs_sem, rs_out, ag_sem, ag_out, col_sem, col_out,
    res_sem, res_out, far_sem, far_out, near_sem, near_out, pass_sem, pass_out,
):
    leaf = lax.axis_index("leaf")
    row = lax.axis_index("row")
    col = lax.axis_index("col")
    z = row // N_X
    x = lax.rem(row, N_X)
    pair = leaf // 2 * 2
    every = range(BATCHES)
    wide = N_COL * BLOCK
    s_top, s_mid = (s_top_0, s_top_1), (s_mid_0, s_mid_1)

    rows_at = {}
    for dz in range(N_Z):
        for dx in range(N_X):
            rows_at[dz, dx] = lax.rem(z + dz, N_Z) * N_X + lax.rem(x + dx, N_X)
    row_offsets = [(dz, dx) for dz in outward(N_Z) for dx in (1, 0)]

    def peers(kind):
        if kind == "top":
            leaves = [(lax.rem(leaf + dy, N_LEAF), dy) for dy in outward(N_LEAF)]
        elif kind == "mid":
            leaves = [(pair + lax.rem(leaf - pair + dy, 2), dy) for dy in (1, 0)]
        else:
            leaves = [(leaf, 0)]
        found = []
        for other, dy in leaves:
            for dz, dx in row_offsets:
                if (dy, dz, dx) != (0, 0, 0):
                    r = rows_at[dz, dx]
                    base = {"top": other, "mid": other - pair, "low": 0}[kind]
                    found.append((base * N_ROW + r, (other, r, col)))
        return found

    group = {k: peers(k) for k in ("top", "mid", "low")}
    own = {"top": leaf * N_ROW + row, "mid": (leaf - pair) * N_ROW + row, "low": row}
    other_cols = [lax.rem(col + d, N_COL) for d in (2, 3, 1)]
    others = [(leaf, row, c) for c in other_cols]
    far_col = lax.rem(col + 2, N_COL)
    near_col = col + 1 - 2 * lax.rem(col, 2)
    far, near = (leaf, row, far_col), (leaf, row, near_col)
    on_diagonal = leaf == col

    def remote(src, dst, send, recv, device):
        return pltpu.make_async_remote_copy(
            src_ref=src, dst_ref=dst, send_sem=send, recv_sem=recv, device_id=device, device_id_type=MESH
        )

    def whole(ref, sem):
        return pltpu.make_async_copy(ref, ref, sem)

    def batch(ref, b):
        return ref[b] if isinstance(ref, tuple) else ref.at[b]

    gathered = [
        (tiles_mid.at[0, 0, 0], tm),
        (inv_mid, im),
        (tiles_low.at[0, 0, 0], tl),
        (inv_low, il),
    ]
    places_of = [(inv_low, il.at[col]), (tiles_low.at[0, 0, 0], tl.at[col]), (inv_mid, im.at[col])]
    places_of += [(tiles_mid.at[0, 0, 0], tm.at[col]), (inv_top, it)]
    copies = [(rhs_low, rl), places_of[0], places_of[1], (rhs_mid, rm), places_of[2], places_of[3], (rhs_top, rt)]
    copies += [places_of[4]]
    loads = [pltpu.make_async_copy(src, dst, load_sem.at[i]) for i, (src, dst) in enumerate(copies)]
    for load in loads:
        load.start()

    barrier = pltpu.get_barrier_semaphore()
    for _, device in group["top"]:
        pl.semaphore_signal(barrier, inc=1, device_id=device, device_id_type=MESH)
    for device in others:
        pl.semaphore_signal(barrier, inc=1, device_id=device, device_id_type=MESH)
    for dy in outward(N_LEAF):
        for dz, dx in row_offsets:
            source = (lax.rem(leaf + dy, N_LEAF), rows_at[dz, dx], leaf)
            if (dy, dz, dx) != (0, 0, 0):
                pl.semaphore_signal(barrier, inc=1, device_id=source, device_id_type=MESH)
            else:

                @pl.when(jnp.logical_not(on_diagonal))
                def _():
                    pl.semaphore_signal(barrier, inc=1, device_id=source, device_id_type=MESH)

    def cut_batches(ref, to):
        for b in every:
            for q in range(N_COL):
                to[b, q * BLOCK : (q + 1) * BLOCK] = ref[q * SHARE + b * BLOCK : q * SHARE + (b + 1) * BLOCK]

    loads[0].wait()
    cut_batches(rl, rl_cut)
    pl.semaphore_wait(barrier, len(group["top"]) + len(others) + TOP - on_diagonal.astype(jnp.int32))

    is_source = col == row // 4
    place_low = lax.rem(row, 4)

    @pl.when(is_source)
    def _():
        for b in every:
            here = x_low.at[b, place_low]
            for _, device in group["low"]:
                remote(rl_cut.at[b], here, start_out.at[b], start_sem.at[b], device).start()
            pltpu.make_async_copy(rl_cut.at[b], here, start_sem.at[b]).start()

    pieces = []
    for i, count in ((0, 4), (1, 8), (2, 2), (3, 4)):
        step = gathered[i][0].shape[0] // count
        pieces += [(i, pl.ds(n * step, step)) for n in range(count)]
    pieces.reverse()

    def gather_far(count=PIECES):
        for _ in range(min(count, len(pieces))):
            i, cut = pieces.pop()
            src, dst = gathered[i]
            remote(src.at[cut], dst.at[col, cut], far_out.at[i], far_sem.at[i], far).start()

    def forward_part(i):
        dst = gathered[i][1].at[far_col]
        whole(dst, far_sem.at[i]).wait()
        remote(dst, dst, pass_out.at[i], pass_sem.at[i], near).start()

    def gathered_all(i):
        part = gathered[i][1].at[0]
        whole(part, near_sem.at[i]).wait()
        whole(part, pass_sem.at[i]).wait()

    for (src, dst), sem, out in ((places_low, all_low), place_sem.at[0], place_out.at[0]), (
        (places_mid, all_mid), place_sem.at[1], place_out.at[1]
    ):
        for device in others:
            remote(src, dst.at[col], out, sem, device).start()
        for n in range(src.shape[3]):
            dst[col, 0, 0, 0, n] = src[0, 0, 0, n]
    for i, (src, dst) in enumerate(gathered):
        remote(src, dst.at[col], near_out.at[i], near_sem.at[i], near).start()
    gather_far()

    def prepare(raw, high, low):
        size = raw.shape[2]
        for c in range(N_COL):
            for p in range(0, size, 512):
                cut = slice(c * size + p, c * size + p + 512)
                high[:, cut], low[:, cut] = split(raw[c, :, p : p + 512])

    def prepare_own(raw, high, low):
        for p in range(0, high.shape[1], 512):
            cut = slice(p, p + 512)
            high[:, cut], low[:, cut] = split(raw[:, cut])

    def prepare_tiles(raw, high, low):
        count = raw.shape[1]
        for c in range(N_COL):
            for n in range(count):
                cut = slice((c * count + n) * TILE, (c * count + n + 1) * TILE)
                high[cut], low[cut] = split(raw[c, n])

    def prepare_own_tiles(raw, high, low):
        for n in range(raw.shape[1]):
            cut = slice(n * TILE, (n + 1) * TILE)
            high[cut], low[cut] = split(raw[col, n])

    loads[1].wait()
    prepare_own(il.at[col], own_low_h, own_low_l)

    def send_shares(stage, b, kind, send, got):
        me = own[kind]
        for k, device in group[kind]:
            remote(send.at[b, k], got.at[b, me], rs_out.at[stage, b], rs_sem.at[stage, b], device).start()
        got[b, me] = send[b, me]

    def sum_shares(stage, b, kind, got):
        whole(got.at[b, pl.ds(0, len(group[kind]))], rs_sem.at[stage, b]).wait()
        return jnp.sum(got[b], axis=0)

    def spread(stage, b, kind, total, ref):
        mine = batch(ref, b).at[own[kind]]
        mine[...] = total
        for _, device in group[kind]:
            remote(mine, mine, ag_out.at[stage, b], ag_sem.at[stage, b], device).start()

    def get_columns(stage, b, kind, ref):
        whole(batch(ref, b).at[pl.ds(0, len(group[kind]))], ag_sem.at[stage, b]).wait()

    def send_col(stage, b, value):
        mine = col_got.at[stage, b, col]
        mine[...] = value
        for device in others:
            remote(mine, mine, col_out.at[stage, b], col_sem.at[stage, b], device).start()

    def get_col(stage, b):
        whole(col_got.at[stage, b, pl.ds(0, N_COL - 1)], col_sem.at[stage, b]).wait()
        got = [col_got[stage, b, c] for c in range(N_COL)]
        return (got[0] + got[1]) + (got[2] + got[3])

    def forward(ref, b, positions, high, low):
        columns = jnp.concatenate(
            [ref[b, p * N_COL : (p + 1) * N_COL].reshape(wide, TILE) for p in range(positions)], axis=1
        )
        return product(columns, high[...], low[...], NT)

    def lift(vector, b, places, high, low, rhs, is_mine, my_place, send, positions):
        count = places.shape[3]
        parts = product(vector, high[...], low[...], NT)
        mine = jnp.where(is_mine, rhs[b], 0.0)
        for p in range(positions):
            value = jnp.where(my_place == p, mine, 0.0)
            for n in range(count):
                value = value - jnp.where(places[0, 0, 0, n] == p, parts[:, n * TILE : (n + 1) * TILE], 0.0)
            send[b, p * N_COL : (p + 1) * N_COL] = value.reshape(N_COL, BLOCK, TILE)

    def lower(ref, b, places, high, low, positions):
        count = places.shape[4]
        picked = [
            batch(ref, b)[c * positions + places[c, 0, 0, 0, n]] for c in range(N_COL) for n in range(count)
        ]
        return product(jnp.concatenate(picked, axis=1), high[...], low[...], NN)

    def backward(value, b, high, low, send):
        part = product(value, high[...], low[...], NN)
        for p in range(high.shape[1] // TILE):
            send[b, p] = part[:, p * TILE : (p + 1) * TILE]

    def own_columns(ref, b):
        return ref[b, pl.ds(pl.multiple_of(col * BLOCK, BLOCK), BLOCK)]

    def send_result(level, b, src, out):
        place = pl.ds(pl.multiple_of(col * SHARE + b * BLOCK, BLOCK), BLOCK)
        for device in others:
            remote(src, out.at[place], res_out.at[level, b], res_sem.at[level, b], device).start()
        out[place] = src[...]

    mid_index = own["mid"]
    mine_mid, place_mid = col == mid_index // 8, lax.rem(mid_index, 8)

    for b in every:
        whole(x_low.at[b], start_sem.at[b]).wait()
        columns = jnp.concatenate([x_low[b, p] for p in range(4)], axis=1)
        send_col(0, b, product(columns, own_low_h[...], own_low_l[...], NT))
    gather_far()
    loads[2].wait()
    prepare_own_tiles(tl, own_tl_h, own_tl_l)
    loads[3].wait()
    cut_batches(rm, rm_cut)
    for b in every:
        low_y[b] = get_col(0, b)
        lift(low_y[b], b, places_low, own_tl_h, own_tl_l, rm_cut, mine_mid, place_mid, send1, 8)
        send_shares(0, b, "mid", send1, got1)
    gather_far()
    loads[4].wait()
    prepare_own(im.at[col], own_mid_h, own_mid_l)
    for b in every:
        spread(0, b, "mid", sum_shares(0, b, "mid", got1), x_mid)
    gather_far()
    loads[5].wait()
    prepare_own_tiles(tm, own_tm_h, own_tm_l)
    loads[6].wait()
    cut_batches(rt, rt_cut)
    for b in every:
        get_columns(0, b, "mid", x_mid)
        send_col(1, b, forward(x_mid, b, 8, own_mid_h, own_mid_l))
    gather_far()
    for b in every:
        mid_y[b] = get_col(1, b)
        lift(mid_y[b], b, places_mid, own_tm_h, own_tm_l, rt_cut, on_diagonal, row, send2, 16)
        send_shares(1, b, "top", send2, got2)
    gather_far()
    loads[7].wait()
    prepare_own(it, top_h, top_l)
    for b in every:
        spread(1, b, "top", sum_shares(1, b, "top", got2), x_top)
    gather_far()
    for b in every:
        get_columns(1, b, "top", x_top)
        send_col(2, b, forward(x_top, b, 16, top_h, top_l))
    gather_far()
    for b in every:
        part = product(get_col(2, b), top_h[...], top_l[...], NN)
        for p in range(N_ROW):
            send3[b, p] = part[:, p * TILE : (p + 1) * TILE].reshape(N_COL, BLOCK, TILE)
        me = own["top"]
        for dz, dx in row_offsets:
            r = rows_at[dz, dx]
            for d in (2, 3, 1, 0):
                q = lax.rem(col + d, N_COL)
                copy = remote(
                    send3.at[b, r, q], got3.at[b, me], rs_out.at[2, b], rs_sem.at[2, b], (col, r, q)
                )
                if (dz, dx, d) != (0, 0, 0):
                    copy.start()
                else:

                    @pl.when(on_diagonal)
                    def _():
                        pltpu.make_async_copy(send3.at[b, r, q], got3.at[b, me], rs_sem.at[2, b]).start()

                    @pl.when(jnp.logical_not(on_diagonal))
                    def _():
                        copy.start()

    gather_far(len(pieces))
    forward_part(0)
    forward_part(1)
    for b in every:
        whole(got3.at[b], rs_sem.at[2, b]).wait()
        spread(2, b, "top", jnp.sum(got3[b], axis=0), s_top)
    for b in every:
        send_result(0, b, batch(s_top, b).at[own["top"]], o_top)
    gathered_all(0)
    prepare_tiles(tm, tm_h, tm_l)
    gathered_all(1)
    prepare(im, mid_h, mid_l)
    for i in range(2):
        whole((all_low, all_mid)[i].at[pl.ds(0, N_COL - 1)], place_sem.at[i]).wait()
    forward_part(2)
    forward_part(3)
    for b in every:
        get_columns(2, b, "top", s_top)
        value = own_columns(mid_y, b) - lower(s_top, b, all_mid, tm_h, tm_l, 16)
        backward(value, b, mid_h, mid_l, send4)
        send_shares(3, b, "mid", send4, got4)
    gathered_all(2)
    prepare_tiles(tl, tl_h, tl_l)
    for b in every:
        spread(3, b, "mid", sum_shares(3, b, "mid", got4), s_mid)
    for b in every:
        send_result(1, b, batch(s_mid, b).at[own["mid"]], o_mid)
    gathered_all(3)
    prepare(il, low_h, low_l)
    for b in every:
        get_columns(3, b, "mid", s_mid)
        value = own_columns(low_y, b) - lower(s_mid, b, all_low, tl_h, tl_l, 8)
        backward(value, b, low_h, low_l, send5)
        send_shares(4, b, "low", send5, got5)
    for b in every:
        tail5[b] = sum_shares(4, b, "low", got5)
        send_result(2, b, tail5.at[b], o_low)

    results = [(o_top, out_top), (o_mid, out_mid), (o_low, out_low)]
    for level, (ref, out) in enumerate(results):
        for b in every:
            whole(ref.at[pl.ds(0, (N_COL - 1) * BLOCK)], res_sem.at[level, b]).wait()
        out[...] = ref[...]

    for b in every:

        @pl.when(is_source)
        def _():
            for _ in group["low"]:
                whole(rl_cut.at[b], start_out.at[b]).wait()

        for level, (ref, _) in enumerate(results):
            whole(ref.at[pl.ds(0, (N_COL - 1) * BLOCK)], res_out.at[level, b]).wait()
        for stage, (kind, send, ref) in enumerate(
            [
                ("mid", send1, x_mid),
                ("top", send2, x_top),
                ("top", None, s_top),
                ("mid", send4, s_mid),
                ("low", send5, None),
            ]
        ):
            count = len(group[kind])
            if send is not None:
                whole(send.at[b, pl.ds(0, count)], rs_out.at[stage, b]).wait()
            if ref is not None:
                whole(batch(ref, b).at[pl.ds(0, count)], ag_out.at[stage, b]).wait()
        whole(got3.at[b, pl.ds(0, TOP - 1)], rs_out.at[2, b]).wait()

        @pl.when(jnp.logical_not(on_diagonal))
        def _():
            whole(got3.at[b, 0], rs_out.at[2, b]).wait()

        for stage in range(3):
            whole(col_got.at[stage, b, pl.ds(0, N_COL - 1)], col_out.at[stage, b]).wait()
    for i, (_, dst) in enumerate(gathered):
        for sem in (far_out, near_out, pass_out):
            whole(dst.at[0], sem.at[i]).wait()
    for i in range(2):
        whole((all_low, all_mid)[i].at[pl.ds(0, N_COL - 1)], place_out.at[i]).wait()


def body(rhs_top, rhs_mid, rhs_low, *others):
    vm = pltpu.VMEM
    wide = N_COL * BLOCK

    def blocks(count):
        return vm((BATCHES, count, BLOCK, TILE), f32)

    def alone(count):
        return [vm((count, BLOCK, TILE), f32)] * BATCHES

    def halves(*shape):
        return [vm(shape, bf16)] * 2

    scratch = [vm((64, TILE), f32)] * 3 + [vm((BATCHES, wide, TILE), f32)] * 3
    scratch += [vm((TILE, 2048), f32)]
    scratch += [vm((N_COL, TILE, size), f32) for size in (1024, 512)]
    scratch += [vm((N_COL, count, TILE, TILE), f32) for count in (4, 2)]
    scratch += [pltpu.SMEM((N_COL, 1, 1, 1, count), jnp.int32) for count in (4, 2)]
    scratch += halves(TILE, 2048) + halves(TILE, 4096) + halves(TILE, 2048) + halves(TILE, 1024) + halves(TILE, 512)
    for count in (16, 8, 4, 2):
        scratch += halves(count * TILE, TILE)
    scratch += [vm((BATCHES, 4, wide, TILE), f32)]
    scratch += [blocks(MID)] * 3 + [blocks(TOP)] * 3 + [vm((BATCHES, N_ROW, N_COL, BLOCK, TILE), f32)]
    scratch += [blocks(TOP)] + alone(TOP) + [blocks(MID)] * 2 + alone(MID)
    scratch += [blocks(LOW)] * 2 + [vm((BATCHES, BLOCK, TILE), f32)]
    scratch += [vm((3, BATCHES, N_COL, wide, TILE), f32)] + [vm((BATCHES, wide, TILE), f32)] * 2
    scratch += [vm((64, TILE), f32)] * 3
    dma = pltpu.SemaphoreType.DMA
    scratch += [dma((8,)), dma((2,)), dma((2,)), dma((BATCHES,)), dma((BATCHES,))]
    scratch += [dma((5, BATCHES)), dma((5, BATCHES)), dma((4, BATCHES)), dma((4, BATCHES))]
    scratch += [dma((3, BATCHES)), dma((3, BATCHES)), dma((3, BATCHES)), dma((3, BATCHES))]
    scratch += [dma((4,))] * 6
    anywhere = pl.BlockSpec(memory_space=pltpu.HBM)
    scalars = pl.BlockSpec(memory_space=pltpu.SMEM)
    out = pl.BlockSpec(memory_space=pltpu.VMEM)
    solved = pl.pallas_call(
        kernel,
        name="solve",
        out_shape=[jax.ShapeDtypeStruct((64, TILE), f32)] * 3,
        in_specs=[anywhere] * 7 + [scalars, anywhere, scalars],
        out_specs=[out] * 3,
        scratch_shapes=scratch,
        compiler_params=pltpu.CompilerParams(
            collective_id=0, has_side_effects=True, vmem_limit_bytes=60 * 1024 * 1024
        ),
    )(rhs_top.T, rhs_mid.T, rhs_low.T, *others)
    return tuple(part.T for part in solved)


def solution(mesh):
    vector = P(("leaf", "row"), None)
    matrix = P(("leaf", "row"), "col")
    tiles = P("leaf", "row", "col", None, None, None)
    places = P("leaf", "row", "col", None)
    return jax.shard_map(
        body,
        mesh=mesh,
        in_specs=(vector, vector, vector, matrix, matrix, matrix, tiles, places, tiles, places),
        out_specs=(vector, vector, vector),
        check_vma=False,
    )
```

time: 127 us -> 124 us (0.976)
  Pallas kernels: 123 us -> 120 us
    pallas_call x1, Pallas kernels: 123 us -> 120 us  [body(): pl.pallas_call(kernel, name='solve', out_shape=[jax.ShapeDtypeStruct((64,...]
where the time goes in v2:
time: 124 us
  Pallas kernels  120 us (97%)
  local copies, waits for them, and re-layouts  2.77 us (2%)
    pallas_call x1, Pallas kernels, body(): pl.pallas_call(kernel, name='solve', out_shape=[jax.ShapeDtypeStruct((64,...  120 us
    unnamed x7, local copies, waits for them, and re-layouts  2.77 us

profile of v2, /device:TPU:1, one launch (start us, length us, event | category | flops | bytes accessed | tf_op | source)
XLA Modules:
  0.0 123.7 jit_solution(2242372129114587560)
XLA Ops:
  0.6 120.3 %solve.1 = (f32[64,128]{1,0:T(8,128)}, f32[64,128]{1,0:T(8,128)}, f32[64,128]{1,0:T(8,128)}) custom-call(f32[64,128]{1,0:T(8,128)} %bitcast.6, f32[64,128]{1,0:T(8,128)} %bitcast.7, f32[64,128]{1,0:T(8,128)} %bitcast.8, f32[128,2048]{1,0:T(8,128)} %inv_top.1, f32[128,1024]{1,0:T(8,128)} %inv_mid.1, f32[128,512]{1,0:T(8,128)} %inv_low.1, ...), custom_call_target="tpu_custom_call" | custom-call | tf_op jit(solution)/shard_map/solve/pallas_call | solution.py:468
  120.9 0.0 copy-start.1
  120.9 1.4 %copy.16 = f32[128,64]{0,1:T(8,128)} copy(f32[128,64]{0,1:T(8,128)} %bitcast.11) | data formatting | bytes 65536
  122.3 0.0 copy-done.1
  122.3 0.0 copy-start
  122.3 0.6 copy.17
  122.9 0.2 copy-done
  123.1 0.6 copy.18
Async XLA Ops:
  120.9 1.4 %copy-start.1 = (f32[64,128]{1,0:T(8,128)S(1)}, f32[64,128]{1,0:T(8,128)}, u32[]{:S(2)}) copy-start(f32[64,128]{1,0:T(8,128)} %get-tuple-element.7) | copy-start | bytes 98308
  122.3 0.8 copy-start

commit v3 on v2

--- a/solution.py
+++ b/solution.py
@@ -91,6 +91,7 @@
     near_col = col + 1 - 2 * lax.rem(col, 2)
     far, near = (leaf, row, far_col), (leaf, row, near_col)
     on_diagonal = leaf == col
+    below = leaf >= col
 
     def remote(src, dst, send, recv, device):
         return pltpu.make_async_remote_copy(
@@ -117,6 +118,9 @@
     for load in loads:
         load.start()
 
+    for ref in (got3, got4, got5):
+        ref[...] = jnp.zeros_like(ref)
+
     barrier = pltpu.get_barrier_semaphore()
     for _, device in group["top"]:
         pl.semaphore_signal(barrier, inc=1, device_id=device, device_id_type=MESH)
@@ -226,8 +230,20 @@
     def spread(stage, b, kind, total, ref):
         mine = batch(ref, b).at[own[kind]]
         mine[...] = total
-        for _, device in group[kind]:
-            remote(mine, mine, ag_out.at[stage, b], ag_sem.at[stage, b], device).start()
+        if stage != 1:
+            for _, device in group[kind]:
+                remote(mine, mine, ag_out.at[stage, b], ag_sem.at[stage, b], device).start()
+            return
+        for other, devices in leaf_groups():
+
+            @pl.when(other >= col)
+            def _():
+                for device in devices:
+                    remote(mine, mine, ag_out.at[stage, b], ag_sem.at[stage, b], device).start()
+
+    def leaf_groups():
+        devices = [device for _, device in group["top"]]
+        return [(devices[at][0], devices[at : at + N_ROW]) for at in range(0, TOP, N_ROW)]
 
     def get_columns(stage, b, kind, ref):
         whole(batch(ref, b).at[pl.ds(0, len(group[kind]))], ag_sem.at[stage, b]).wait()
@@ -321,38 +337,58 @@
         spread(1, b, "top", sum_shares(1, b, "top", got2), x_top)
     gather_far()
     for b in every:
-        get_columns(1, b, "top", x_top)
-        send_col(2, b, forward(x_top, b, 16, top_h, top_l))
-    gather_far()
-    for b in every:
-        part = product(get_col(2, b), top_h[...], top_l[...], NN)
-        for p in range(N_ROW):
-            send3[b, p] = part[:, p * TILE : (p + 1) * TILE].reshape(N_COL, BLOCK, TILE)
-        me = own["top"]
-        for dz, dx in row_offsets:
-            r = rows_at[dz, dx]
-            for d in (2, 3, 1, 0):
-                q = lax.rem(col + d, N_COL)
-                copy = remote(
-                    send3.at[b, r, q], got3.at[b, me], rs_out.at[2, b], rs_sem.at[2, b], (col, r, q)
-                )
-                if (dz, dx, d) != (0, 0, 0):
-                    copy.start()
-                else:
-
-                    @pl.when(on_diagonal)
-                    def _():
-                        pltpu.make_async_copy(send3.at[b, r, q], got3.at[b, me], rs_sem.at[2, b]).start()
-
-                    @pl.when(jnp.logical_not(on_diagonal))
-                    def _():
+        mine = col_got.at[2, b, col]
+
+        @pl.when(below)
+        def _():
+            get_columns(1, b, "top", x_top)
+            mine[...] = forward(x_top, b, 16, top_h, top_l)
+
+        @pl.when(jnp.logical_not(below))
+        def _():
+            mine[...] = jnp.zeros_like(mine)
+
+        for device in others:
+            remote(mine, mine, col_out.at[2, b], col_sem.at[2, b], device).start()
+    gather_far()
+    for b in every:
+        top_y = get_col(2, b)
+
+        @pl.when(below)
+        def _():
+            part = product(top_y, top_h[...], top_l[...], NN)
+            for p in range(N_ROW):
+                send3[b, p] = part[:, p * TILE : (p + 1) * TILE].reshape(N_COL, BLOCK, TILE)
+            me = own["top"]
+            for dz, dx in row_offsets:
+                r = rows_at[dz, dx]
+                for d in (2, 3, 1, 0):
+                    q = lax.rem(col + d, N_COL)
+                    copy = remote(
+                        send3.at[b, r, q], got3.at[b, me], rs_out.at[2, b], rs_sem.at[2, b], (col, r, q)
+                    )
+                    if (dz, dx, d) != (0, 0, 0):
                         copy.start()
+                    else:
+
+                        @pl.when(on_diagonal)
+                        def _():
+                            pltpu.make_async_copy(send3.at[b, r, q], got3.at[b, me], rs_sem.at[2, b]).start()
+
+                        @pl.when(jnp.logical_not(on_diagonal))
+                        def _():
+                            copy.start()
 
     gather_far(len(pieces))
     forward_part(0)
     forward_part(1)
     for b in every:
-        whole(got3.at[b], rs_sem.at[2, b]).wait()
+        for leaves in range(1, N_LEAF + 1):
+
+            @pl.when(N_LEAF - leaf == leaves)
+            def _():
+                whole(got3.at[b, pl.ds(0, leaves * N_ROW)], rs_sem.at[2, b]).wait()
+
         spread(2, b, "top", jnp.sum(got3[b], axis=0), s_top)
     for b in every:
         send_result(0, b, batch(s_top, b).at[own["top"]], o_top)
@@ -404,7 +440,7 @@
         for stage, (kind, send, ref) in enumerate(
             [
                 ("mid", send1, x_mid),
-                ("top", send2, x_top),
+                ("top", send2, None),
                 ("top", None, s_top),
                 ("mid", send4, s_mid),
                 ("low", send5, None),
@@ -415,11 +451,22 @@
                 whole(send.at[b, pl.ds(0, count)], rs_out.at[stage, b]).wait()
             if ref is not None:
                 whole(batch(ref, b).at[pl.ds(0, count)], ag_out.at[stage, b]).wait()
-        whole(got3.at[b, pl.ds(0, TOP - 1)], rs_out.at[2, b]).wait()
-
-        @pl.when(jnp.logical_not(on_diagonal))
+
+        @pl.when(on_diagonal)
         def _():
-            whole(got3.at[b, 0], rs_out.at[2, b]).wait()
+            whole(got3.at[b, pl.ds(0, TOP - 1)], rs_out.at[2, b]).wait()
+
+        @pl.when(leaf > col)
+        def _():
+            whole(got3.at[b], rs_out.at[2, b]).wait()
+
+        for leaves in range(1, N_LEAF + 1):
+            for mine in (0, 1):
+                sent = leaves * N_ROW - mine
+
+                @pl.when(jnp.logical_and(N_LEAF - col == leaves, below if mine else jnp.logical_not(below)))
+                def _():
+                    whole(x_top.at[b, pl.ds(0, sent)], ag_out.at[1, b]).wait()
 
         for stage in range(3):
             whole(col_got.at[stage, b, pl.ds(0, N_COL - 1)], col_out.at[stage, b]).wait()

time: 124 us -> 122 us (0.984)
  Pallas kernels: 120 us -> 118 us
    pallas_call x1, Pallas kernels: 120 us -> 118 us  [body(): pl.pallas_call(kernel, name='solve', out_shape=[jax.ShapeDtypeStruct((64,...]
where the time goes in v3:
time: 122 us; the launch traced here: 121 us
  Pallas kernels  118 us (97%)
  local copies, waits for them, and re-layouts  2.77 us (2%)
    pallas_call x1, Pallas kernels, body(): pl.pallas_call(kernel, name='solve', out_shape=[jax.ShapeDtypeStruct((64,...  118 us
    unnamed x7, local copies, waits for them, and re-layouts  2.77 us

profile of v3, /device:TPU:1, one launch (start us, length us, event | category | flops | bytes accessed | tf_op | source)
XLA Modules:
  0.0 121.3 jit_solution(2417018184518211547)
XLA Ops:
  0.6 117.9 %solve.1 = (f32[64,128]{1,0:T(8,128)}, f32[64,128]{1,0:T(8,128)}, f32[64,128]{1,0:T(8,128)}) custom-call(f32[64,128]{1,0:T(8,128)} %bitcast.6, f32[64,128]{1,0:T(8,128)} %bitcast.7, f32[64,128]{1,0:T(8,128)} %bitcast.8, f32[128,2048]{1,0:T(8,128)} %inv_top.1, f32[128,1024]{1,0:T(8,128)} %inv_mid.1, f32[128,512]{1,0:T(8,128)} %inv_low.1, ...), custom_call_target="tpu_custom_call" | custom-call | tf_op jit(solution)/shard_map/solve/pallas_call | solution.py:515
  118.5 0.0 copy-start.1
  118.5 1.4 %copy.16 = f32[128,64]{0,1:T(8,128)} copy(f32[128,64]{0,1:T(8,128)} %bitcast.11) | data formatting | bytes 65536
  119.9 0.0 copy-done.1
  119.9 0.0 copy-start
  119.9 0.6 copy.17
  120.5 0.2 copy-done
  120.7 0.6 copy.18
Async XLA Ops:
  118.5 1.4 %copy-start.1 = (f32[64,128]{1,0:T(8,128)S(1)}, f32[64,128]{1,0:T(8,128)}, u32[]{:S(2)}) copy-start(f32[64,128]{1,0:T(8,128)} %get-tuple-element.7) | copy-start | bytes 98308
  119.9 0.8 copy-start
